TPU v7x, 256 devices: a whole 4x4x8 slice. The times are simulated.
256 devices in a mesh: cplx: 8 (over y, core), grp: 32 (over z, x).
Axes of the slice: x: 4, y: 4, z: 8, core: 2. Of those that a mesh axis runs over, the one named last changes fastest.
Arguments:
- sequence_stack: bfloat16 [8, 512, 256, 256], P('cplx', 'grp'), may hold values from -6 to 6
- depths: int32 [8], replicated, may hold values from 64 to 512, as said below
- standardize_factor: float32 [256], replicated, may hold values from 0.1 to 1.9
- standardize_shift: float32 [256], replicated, may hold values from -1.5 to 1.5
- input_weight: bfloat16 [256, 1024], P(None, 'cplx')
- sigmoid_shift: float32 [256], replicated, may hold values from -4 to 4
- result_matrix: bfloat16 [256, 256], P('cplx'), may hold values from -0.375 to 0.375
- result_shift: float32 [256], replicated, may hold values from -1.5 to 1.5
Outputs:
- msa_out: bfloat16 [8, 512, 256, 256], P('cplx', 'grp')
Inputs may be any that keep to these rules, and one draw needn't show every extreme that they name: `depths`: one complex has exactly 512 rows and one exactly 64.
All inputs are finite; a program needn't handle non-finite values.
Results may differ from a plain program's by a relative error of at most 0.0034.
The roundings to bfloat16 on the way count: a program that leaves them out, or rounds other values in their place, can miss the bound.
Values may be sent and summed in bfloat16 or wider, within the bound.
No kernel may reach another device: no remote copies, remote signals or barrier semaphores. Data moves between devices by JAX's collectives and lax.ppermute only.
A program may use at most 192 MiB of HBM per device.

v0:
```python
from functools import partial
import math

import jax
import jax.numpy as jnp
from jax import lax
from jax.experimental import pallas as pl
from jax.experimental.pallas import tpu as pltpu
from jax.sharding import PartitionSpec as P

FOCUS_PATHS = 8
TILE = 16
SOFT_ROWS = 64
VMEM_LIMIT = 48 * 1024 * 1024
WIDTHS = ((4, 4), (4, 4))


def swap_matrix():
    to = lax.broadcasted_iota(jnp.int32, (TILE * TILE, TILE * TILE), 0)
    come = lax.broadcasted_iota(jnp.int32, (TILE * TILE, TILE * TILE), 1)
    return ((to % TILE) * TILE + to // TILE == come).astype(jnp.bfloat16)


def swap_tokens(permutation, tokens):
    return jnp.dot(permutation, tokens, preferred_element_type=jnp.float32).astype(jnp.bfloat16)


def pack_kernel(x_ref, o_ref):
    rows, homes, channels = x_ref.shape
    permutation = swap_matrix()
    for first in range(0, homes, TILE):
        tokens = x_ref[:, first : first + TILE, :].reshape(TILE * TILE, channels)
        swapped = swap_tokens(permutation, tokens)
        o_ref[first : first + TILE, 0] = swapped.reshape(TILE, rows, channels)


def unpack_kernel(y_ref, *rest):
    o_ref = rest[-1]
    rows, homes, channels = o_ref.shape
    permutation = swap_matrix()
    for first in range(0, homes, TILE):
        tokens = y_ref[first : first + TILE, 0].reshape(TILE * TILE, channels)
        swapped = swap_tokens(permutation, tokens)
        o_ref[:, first : first + TILE, :] = swapped.reshape(rows, TILE, channels)


def pack(rows, start, width, homes):
    complex_rows, _, channels = rows.shape
    return pl.pallas_call(
        pack_kernel,
        grid=(width,),
        in_specs=[pl.BlockSpec((complex_rows, homes, channels), lambda j: (0, start + j, 0))],
        out_specs=pl.BlockSpec((homes, 1, complex_rows, channels), lambda j: (0, j, 0, 0)),
        out_shape=jax.ShapeDtypeStruct((homes, width, complex_rows, channels), jnp.bfloat16),
        compiler_params=pltpu.CompilerParams(vmem_limit_bytes=VMEM_LIMIT),
        name="pack_columns",
    )(rows)


def unpack(returned, before, start, columns):
    homes, width, complex_rows, channels = returned.shape
    operands = [returned]
    in_specs = [pl.BlockSpec((homes, 1, complex_rows, channels), lambda j: (0, j, 0, 0))]
    aliases = {}
    if before is not None:
        operands.append(before)
        in_specs.append(pl.BlockSpec(memory_space=pl.ANY))
        aliases = {1: 0}
    return pl.pallas_call(
        unpack_kernel,
        grid=(width,),
        in_specs=in_specs,
        out_specs=pl.BlockSpec((complex_rows, homes, channels), lambda j: (0, start + j, 0)),
        out_shape=jax.ShapeDtypeStruct((complex_rows, columns, channels), jnp.bfloat16),
        input_output_aliases=aliases,
        compiler_params=pltpu.CompilerParams(vmem_limit_bytes=VMEM_LIMIT),
        name="unpack_columns",
    )(*operands)


def column_kernel(
    depth_ref, x_ref, parts_ref, result_ref, norm_ref, sigmoid_ref, shift_ref, o_ref,
    weight_ref, packed_ref, scores_ref, soft_ref
):
    ranks, _, rows, channels = x_ref.shape
    seq_rows = ranks * rows
    path_dimension = channels // FOCUS_PATHS
    depth = depth_ref[0]

    @pl.when(pl.program_id(0) == 0)
    def _():
        width = parts_ref.shape[2]
        for part in range(parts_ref.shape[0]):
            weight_ref[:, part * width : (part + 1) * width] = parts_ref[part]

    values = x_ref[:, 0].reshape(seq_rows, channels).astype(jnp.float32)
    average = jnp.mean(values, -1, keepdims=True)
    centred = values - average
    variance = jnp.mean(jnp.square(centred), -1, keepdims=True)
    normed = (
        centred * lax.rsqrt(variance + 1e-05) * norm_ref[0:1] + norm_ref[1:2]
    ).astype(jnp.bfloat16)
    product = jnp.dot(normed, weight_ref[...], preferred_element_type=jnp.float32)
    packed_ref[:, : 3 * channels] = product[:, : 3 * channels].astype(jnp.bfloat16)
    gates = jax.nn.sigmoid(product[:, 3 * channels :] + sigmoid_ref[...])
    packed_ref[:, 3 * channels :] = gates.astype(jnp.bfloat16)

    keys_t = packed_ref[:, channels : 2 * channels].T
    dead = lax.broadcasted_iota(jnp.int32, (1, seq_rows), 1) >= depth
    head_of = lax.broadcasted_iota(jnp.int32, (1, channels), 1) // path_dimension
    scaling = math.log2(math.e) / math.sqrt(path_dimension)

    def score(head):
        queries = packed_ref[:, :channels]
        own = jnp.where(head_of == head, queries, jnp.zeros_like(queries))
        scores_ref[head % 2] = jnp.dot(own, keys_t, preferred_element_type=jnp.float32)

    def soften(head):
        for first in range(0, seq_rows, SOFT_ROWS):
            scores = jnp.where(dead, -1e30, scores_ref[head % 2, first : first + SOFT_ROWS])
            row_top = jnp.max(scores, -1, keepdims=True) * scaling
            exponent = jnp.exp2(scores * scaling - row_top)
            total = jnp.sum(exponent, -1, keepdims=True)
            soft_ref[head % 2, first : first + SOFT_ROWS] = (exponent * (1.0 / total)).astype(
                jnp.bfloat16
            )

    half = channels // 2
    mixtures = [jnp.zeros((seq_rows, half), jnp.float32)] * 2

    def mix(head):
        side = head * path_dimension // half
        value_rows = packed_ref[:, 2 * channels + side * half : 2 * channels + (side + 1) * half]
        mixed = jnp.dot(soft_ref[head % 2], value_rows, preferred_element_type=jnp.float32)
        own = head_of[:, side * half : (side + 1) * half] == head
        mixtures[side] = jnp.where(own, mixed, mixtures[side])

    score(0)
    for head in range(FOCUS_PATHS):
        if head + 1 < FOCUS_PATHS:
            score(head + 1)
        soften(head)
        if head > 0:
            mix(head - 1)
    mix(FOCUS_PATHS - 1)

    gate_rows = packed_ref[:, 3 * channels :].astype(jnp.float32)
    gated = (gate_rows * jnp.concatenate(mixtures, 1)).astype(jnp.bfloat16)
    update = jnp.dot(gated, result_ref[...], preferred_element_type=jnp.float32) + shift_ref[...]
    live = lax.broadcasted_iota(jnp.int32, (seq_rows, 1), 0) < depth
    update = jnp.where(live, 1.0, 0.0) * update
    changed = x_ref[:, 0].reshape(seq_rows, channels).astype(jnp.float32) + update
    o_ref[:, 0] = changed.astype(jnp.bfloat16).reshape(ranks, rows, channels)


def attend(arrived, own_depth, parts, result, norm, sigmoid, shift):
    ranks, per, rows, channels = arrived.shape
    seq_rows = ranks * rows
    whole = lambda a: pl.BlockSpec(a.shape, lambda i, *_: (0,) * a.ndim)
    column = pl.BlockSpec((ranks, 1, rows, channels), lambda i, *_: (0, i, 0, 0))
    return pl.pallas_call(
        column_kernel,
        grid_spec=pltpu.PrefetchScalarGridSpec(
            num_scalar_prefetch=1,
            grid=(per,),
            in_specs=[column] + [whole(a) for a in (parts, result, norm, sigmoid, shift)],
            out_specs=column,
            scratch_shapes=[
                pltpu.VMEM((channels, 4 * channels), jnp.bfloat16),
                pltpu.VMEM((seq_rows, 4 * channels), jnp.bfloat16),
                pltpu.VMEM((2, seq_rows, seq_rows), jnp.float32),
                pltpu.VMEM((2, seq_rows, seq_rows), jnp.bfloat16),
            ],
        ),
        out_shape=jax.ShapeDtypeStruct(arrived.shape, jnp.bfloat16),
        compiler_params=pltpu.CompilerParams(vmem_limit_bytes=VMEM_LIMIT),
        cost_estimate=pl.CostEstimate(
            flops=per * seq_rows * channels * (10 * channels + 4 * FOCUS_PATHS * seq_rows),
            bytes_accessed=4 * per * seq_rows * channels,
            transcendentals=per * FOCUS_PATHS * seq_rows * seq_rows,
        ),
        name="attend_columns",
    )(own_depth, arrived, parts, result, norm, sigmoid, shift)


def exchange(blocks):
    return lax.all_to_all(blocks, "grp", split_axis=0, concat_axis=0, tiled=True)


def chunked(rows, own_depth, gathered, vectors, homes, widths):
    _, columns, channels = rows.shape
    later, gathered = lax.optimization_barrier((rows, gathered))
    parts = gathered[:, :channels]
    result = gathered[:, channels:].reshape(channels, channels)
    starts = [sum(widths[:i]) for i in range(len(widths))]
    arrived = [
        exchange(pack(later if s else rows, s, w, homes)) for s, w in zip(starts, widths)
    ]
    out = None
    for start, blocks in zip(starts, arrived):
        done = exchange(attend(blocks, own_depth, parts, result, *vectors))
        out = unpack(done, out, start, columns)
    return out


def shards(
    sequence_stack,
    depths,
    standardize_factor,
    standardize_shift,
    input_weight,
    sigmoid_shift,
    result_matrix,
    result_shift,
):
    rows = sequence_stack[0]
    complex_rows, columns, channels = rows.shape
    homes = lax.axis_size("grp")
    team = lax.axis_index("cplx")
    teams = lax.axis_size("cplx")
    own_depth = lax.dynamic_slice(depths, (team,), (1,))
    norm = jnp.stack([standardize_factor, standardize_shift])
    vectors = (norm, sigmoid_shift[None], result_shift[None])
    width = input_weight.shape[1]
    both = jnp.concatenate([input_weight, result_matrix.reshape(-1, width)], axis=0)
    other = lax.ppermute(both, "cplx", [(c, c ^ 1) for c in range(teams)])
    own_core = [list(range(core, teams, 2)) for core in range(2)]

    def run(core, rows, both, other):
        pair = jnp.stack([both, other] if core == 0 else [other, both])
        gathered = lax.all_gather(pair, "cplx", axis=0, tiled=True, axis_index_groups=own_core)
        if core == 1:
            rows, gathered = lax.optimization_barrier((rows, gathered))
        return chunked(rows, own_depth, gathered, vectors, homes, WIDTHS[core])

    return lax.cond(team % 2 == 0, partial(run, 0), partial(run, 1), rows, both, other)[None]


def solution(mesh):
    placed = (
        P("cplx", "grp", None, None),
        P(),
        P(),
        P(),
        P(None, "cplx"),
        P(),
        P("cplx", None),
        P(),
    )
    return jax.shard_map(
        shards, mesh=mesh, in_specs=placed, out_specs=P("cplx", "grp", None, None), check_vma=False
    )
```

profile of v0, /device:TPU:1, one launch (start us, length us, event | category | flops | bytes accessed | tf_op | source)
XLA Modules:
  0.0 141.8 jit_solution(3746727715377663534)
XLA Ops:
  0.0 0.7 reshape.9
  0.7 0.8 constant_dynamic-update-slice_fusion.1
  1.6 3.3 %collective-permute-start = (bf16[320,128]{1,0:T(8,128)(2,1)S(1)}, bf16[320,128]{1,0:T(8,128)(2,1)S(1)}, u32[]{:S(2)}, u32[]{:S(2)}) collective-permute-start(bf16[320,128]{1,0:T(8,128)(2,1)S(1)} %constant_dynamic-update-slice_fusion), channel_id=1, source_target_pairs={{0,32},{32,0},{64,96},{96,64},{128,160},{160,128},{192,224},{224,1... | collective-permute-start | bytes 245768 | tf_op jit(solution)/shard_map/ppermute | solution.py:226
  4.9 1.3 dynamic_slice.3
  6.2 0.7 pad_maximum_fusion.2
  6.9 0.0 collective-permute-done
  6.9 134.8 %conditional.1 = (bf16[1,16,256,256]{3,2,1,0:T(8,128)(2,1)}) conditional(s32[]{:T(128)} %convert_element_type.3, (bf16[320,128]{1,0:T(8,128)(2,1)S(1)}, bf16[320,128]{1,0:T(8,128)(2,1)S(1)}, bf16[16,256,256]{2,1,0:T(8,128)(2,1)}, s32[1]{0:T(128)}, f32[2,256]{1,0:T(2,128)S(1)}, /*index=5*/f32[1,256]{1,0:T(1,128)}, f32[1,256]{1,0:T(1,128)}) %tuple.25, ...), branch_computations={%region_0.1_spmd, %region_1.2_spmd} | conditional | flops 19864305664 | bytes 31301960 | solution.py:236
  7.0 10.9 %all_gather.4 = bf16[8,320,128]{2,1,0:T(8,128)(2,1)} all-gather(bf16[2,320,128]{2,1,0:T(8,128)(2,1)S(1)} %pad_maximum_fusion), channel_id=1, replica_groups={{0,64,128,192},{32,96,160,224},{1,65,129,193},{33,97,161,225},{2,66,130..., dimensions={0}, use_global_device_ids=true | all-gather | bytes 819200 | tf_op jit(solution)/shard_map/cond/branch_0_fun/all_gather | solution.py:231
  17.9 0.0 copy-start
  17.9 4.0 %pack_columns.5 = bf16[32,4,16,256]{3,2,1,0:T(8,128)(2,1)} custom-call(bf16[16,256,256]{2,1,0:T(8,128)(2,1)} %get-tuple-element.46.x_ref), custom_call_target="tpu_custom_call" | custom-call | tf_op jit(solution)/shard_map/cond/branch_0_fun/pack_columns/pallas_call | solution.py:49
  21.9 9.8 %all-to-all-start.2 = ((bf16[32,4,16,256]{3,2,1,0:T(8,128)(2,1)}), bf16[32,4,16,256]{3,2,1,0:T(8,128)(2,1)S(1)}, u32[]{:S(2)}, u32[]{:S(2)}) async-start(bf16[32,4,16,256]{3,2,1,0:T(8,128)(2,1)} %pack_columns.5), calls=%async_computation.2 | async-start | bytes 2097152 | tf_op jit(solution)/shard_map/cond/branch_0_fun/all_to_all | solution.py:187
  31.7 0.0 copy-done
  31.7 2.2 %pack_columns.4 = bf16[32,4,16,256]{3,2,1,0:T(8,128)(2,1)} custom-call(bf16[16,256,256]{2,1,0:T(8,128)(2,1)S(1)} %copy-done), custom_call_target="tpu_custom_call" | custom-call | tf_op jit(solution)/shard_map/cond/branch_0_fun/pack_columns/pallas_call | solution.py:49
  33.9 0.0 copy-start.2
  33.9 0.0 slice-start
  33.9 0.0 copy-start.6
  33.9 0.0 copy-start.8
  33.9 15.8 %all-to-all-done.2.x_ref = bf16[32,4,16,256]{3,2,1,0:T(8,128)(2,1)S(1)} async-done(((bf16[32,4,16,256]{3,2,1,0:T(8,128)(2,1)}), bf16[32,4,16,256]{3,2,1,0:T(8,128)(2,1)S(1)}, u32[]{:S(2)}, u32[]{:S(2)}) %all-to-all-start.2) | async-done | bytes 1048608 | tf_op jit(solution)/shard_map/cond/branch_0_fun/all_to_all | solution.py:187
  49.7 5.2 %all-to-all-start = ((bf16[32,4,16,256]{3,2,1,0:T(8,128)(2,1)}), bf16[32,4,16,256]{3,2,1,0:T(8,128)(2,1)S(1)}, u32[]{:S(2)}, u32[]{:S(2)}) async-start(bf16[32,4,16,256]{3,2,1,0:T(8,128)(2,1)} %pack_columns.4), calls=%async_computation | async-start | bytes 2097152 | tf_op jit(solution)/shard_map/cond/branch_0_fun/all_to_all | solution.py:187
  55.0 0.0 copy-done.2
  55.0 0.0 slice-done
  55.1 0.0 copy-done.6
  55.1 0.0 copy-done.8
  55.1 18.3 %attend_columns.5 = bf16[32,4,16,256]{3,2,1,0:T(8,128)(2,1)} custom-call(s32[1]{0:T(128)} %get-tuple-element.37.depth_ref, bf16[32,4,16,256]{3,2,1,0:T(8,128)(2,1)S(1)} %all-to-all-done.2.x_ref, bf16[8,256,128]{2,1,0:T(8,128)(2,1)S(1)} %slice.8.parts_ref, bf16[256,256]{1,0:T(8,128)(2,1)S(1)} %reshape.6.result_ref, f32[2,256]{1,0:T(2,128)S(1)} %get-tuple-element.43.norm_ref, ...), custom_call_target="tpu_custom_call" | custom-call | flops 9932111872 | bytes 2097152 | tf_op jit(solution)/shard_map/cond/branch_0_fun/attend_columns/pallas_call | solution.py:161
  73.4 3.7 %all-to-all-done.x_ref = bf16[32,4,16,256]{3,2,1,0:T(8,128)(2,1)S(1)} async-done(((bf16[32,4,16,256]{3,2,1,0:T(8,128)(2,1)}), bf16[32,4,16,256]{3,2,1,0:T(8,128)(2,1)S(1)}, u32[]{:S(2)}, u32[]{:S(2)}) %all-to-all-start) | async-done | bytes 1048608 | tf_op jit(solution)/shard_map/cond/branch_0_fun/all_to_all | solution.py:187
  77.0 5.5 %all-to-all-start.3 = ((bf16[32,4,16,256]{3,2,1,0:T(8,128)(2,1)}), bf16[32,4,16,256]{3,2,1,0:T(8,128)(2,1)S(1)}, u32[]{:S(2)}, u32[]{:S(2)}) async-start(bf16[32,4,16,256]{3,2,1,0:T(8,128)(2,1)} %attend_columns.5), calls=%async_computation.3 | async-start | bytes 2097152 | tf_op jit(solution)/shard_map/cond/branch_0_fun/all_to_all | solution.py:187
  82.6 18.3 %attend_columns.4 = bf16[32,4,16,256]{3,2,1,0:T(8,128)(2,1)} custom-call(s32[1]{0:T(128)} %get-tuple-element.37.depth_ref, bf16[32,4,16,256]{3,2,1,0:T(8,128)(2,1)S(1)} %all-to-all-done.x_ref, bf16[8,256,128]{2,1,0:T(8,128)(2,1)S(1)} %slice.8.parts_ref, bf16[256,256]{1,0:T(8,128)(2,1)S(1)} %reshape.6.result_ref, f32[2,256]{1,0:T(2,128)S(1)} %get-tuple-element.43.norm_ref, ...), custom_call_target="tpu_custom_call" | custom-call | flops 9932111872 | bytes 2097152 | tf_op jit(solution)/shard_map/cond/branch_0_fun/attend_columns/pallas_call | solution.py:161
  100.8 6.5 %all-to-all-done.3.y_ref = bf16[32,4,16,256]{3,2,1,0:T(8,128)(2,1)S(1)} async-done(((bf16[32,4,16,256]{3,2,1,0:T(8,128)(2,1)}), bf16[32,4,16,256]{3,2,1,0:T(8,128)(2,1)S(1)}, u32[]{:S(2)}, u32[]{:S(2)}) %all-to-all-start.3) | async-done | bytes 1048608 | tf_op jit(solution)/shard_map/cond/branch_0_fun/all_to_all | solution.py:187
  107.4 5.2 %all-to-all-start.1 = ((bf16[32,4,16,256]{3,2,1,0:T(8,128)(2,1)}), bf16[32,4,16,256]{3,2,1,0:T(8,128)(2,1)S(1)}, u32[]{:S(2)}, u32[]{:S(2)}) async-start(bf16[32,4,16,256]{3,2,1,0:T(8,128)(2,1)} %attend_columns.4), calls=%async_computation.1 | async-start | bytes 2097152 | tf_op jit(solution)/shard_map/cond/branch_0_fun/all_to_all | solution.py:187
  112.6 2.2 %unpack_columns.4.rest_0_ = bf16[16,256,256]{2,1,0:T(8,128)(2,1)} custom-call(bf16[32,4,16,256]{3,2,1,0:T(8,128)(2,1)S(1)} %all-to-all-done.3.y_ref), custom_call_target="tpu_custom_call" | custom-call | tf_op jit(solution)/shard_map/cond/branch_0_fun/unpack_columns/pallas_call | solution.py:69
  114.8 24.7 %all-to-all-done.1.y_ref = bf16[32,4,16,256]{3,2,1,0:T(8,128)(2,1)S(1)} async-done(((bf16[32,4,16,256]{3,2,1,0:T(8,128)(2,1)}), bf16[32,4,16,256]{3,2,1,0:T(8,128)(2,1)S(1)}, u32[]{:S(2)}, u32[]{:S(2)}) %all-to-all-start.1) | async-done | bytes 1048608 | tf_op jit(solution)/shard_map/cond/branch_0_fun/all_to_all | solution.py:187
  139.6 2.2 %unpack_columns.5 = bf16[16,256,256]{2,1,0:T(8,128)(2,1)} custom-call(bf16[32,4,16,256]{3,2,1,0:T(8,128)(2,1)S(1)} %all-to-all-done.1.y_ref, bf16[16,256,256]{2,1,0:T(8,128)(2,1)} %unpack_columns.4.rest_0_), custom_call_target="tpu_custom_call", output_to_operand_aliasing={{}: (1, {})} | custom-call | tf_op jit(solution)/shard_map/cond/branch_0_fun/unpack_columns/pallas_call | solution.py:69
  (4 shorter events, 0.1 us)
Async XLA Ops:
  1.6 5.3 %collective-permute-start = (bf16[320,128]{1,0:T(8,128)(2,1)S(1)}, bf16[320,128]{1,0:T(8,128)(2,1)S(1)}, u32[]{:S(2)}, u32[]{:S(2)}) collective-permute-start(bf16[320,128]{1,0:T(8,128)(2,1)S(1)} %constant_dynamic-update-slice_fusion), channel_id=1, source_target_pairs={{0,32},{32,0},{64,96},{96,64},{128,160},{160,128},{192,224},{224,1... | collective-permute-start | bytes 245768 | tf_op jit(solution)/shard_map/ppermute | solution.py:226
  17.9 13.9 %copy-start = (bf16[16,256,256]{2,1,0:T(8,128)(2,1)S(1)}, bf16[16,256,256]{2,1,0:T(8,128)(2,1)}, u32[]{:S(2)}) copy-start(bf16[16,256,256]{2,1,0:T(8,128)(2,1)} %get-tuple-element.46.x_ref) | copy-start | bytes 6291460 | tf_op jit(solution)/shard_map/cond
  21.9 27.8 %all-to-all-start.2 = ((bf16[32,4,16,256]{3,2,1,0:T(8,128)(2,1)}), bf16[32,4,16,256]{3,2,1,0:T(8,128)(2,1)S(1)}, u32[]{:S(2)}, u32[]{:S(2)}) async-start(bf16[32,4,16,256]{3,2,1,0:T(8,128)(2,1)} %pack_columns.5), calls=%async_computation.2 | async-start | bytes 2097152 | tf_op jit(solution)/shard_map/cond/branch_0_fun/all_to_all | solution.py:187
  33.9 21.0 %copy-start.2 = (bf16[8,320,128]{2,1,0:T(8,128)(2,1)S(1)}, bf16[8,320,128]{2,1,0:T(8,128)(2,1)}, u32[]{:S(2)}) copy-start(bf16[8,320,128]{2,1,0:T(8,128)(2,1)} %all_gather.4) | copy-start | bytes 1966084 | tf_op jit(solution)/shard_map/cond
  33.9 21.1 %slice-start = ((bf16[8,320,128]{2,1,0:T(8,128)(2,1)}), bf16[8,64,128]{2,1,0:T(8,128)(2,1)S(1)}, s32[]{:S(2)}) async-start(bf16[8,320,128]{2,1,0:T(8,128)(2,1)} %all_gather.4), calls=%async_computation.8 | async-start | bytes 262144 | tf_op jit(solution)/shard_map/cond/branch_0_fun/slice | solution.py:194
  33.9 21.1 %copy-start.6 = (f32[1,256]{1,0:T(1,128)S(1)}, f32[1,256]{1,0:T(1,128)}, u32[]{:S(2)}) copy-start(f32[1,256]{1,0:T(1,128)} %get-tuple-element.44.sigmoid_ref) | copy-start | bytes 3076 | tf_op jit(solution)/shard_map/cond
  33.9 21.1 %copy-start.8 = (f32[1,256]{1,0:T(1,128)S(1)}, f32[1,256]{1,0:T(1,128)}, u32[]{:S(2)}) copy-start(f32[1,256]{1,0:T(1,128)} %get-tuple-element.45.shift_ref) | copy-start | bytes 3076 | tf_op jit(solution)/shard_map/cond
  49.7 27.3 %all-to-all-start = ((bf16[32,4,16,256]{3,2,1,0:T(8,128)(2,1)}), bf16[32,4,16,256]{3,2,1,0:T(8,128)(2,1)S(1)}, u32[]{:S(2)}, u32[]{:S(2)}) async-start(bf16[32,4,16,256]{3,2,1,0:T(8,128)(2,1)} %pack_columns.4), calls=%async_computation | async-start | bytes 2097152 | tf_op jit(solution)/shard_map/cond/branch_0_fun/all_to_all | solution.py:187
  77.0 30.3 %all-to-all-start.3 = ((bf16[32,4,16,256]{3,2,1,0:T(8,128)(2,1)}), bf16[32,4,16,256]{3,2,1,0:T(8,128)(2,1)S(1)}, u32[]{:S(2)}, u32[]{:S(2)}) async-start(bf16[32,4,16,256]{3,2,1,0:T(8,128)(2,1)} %attend_columns.5), calls=%async_computation.3 | async-start | bytes 2097152 | tf_op jit(solution)/shard_map/cond/branch_0_fun/all_to_all | solution.py:187
  107.4 32.2 %all-to-all-start.1 = ((bf16[32,4,16,256]{3,2,1,0:T(8,128)(2,1)}), bf16[32,4,16,256]{3,2,1,0:T(8,128)(2,1)S(1)}, u32[]{:S(2)}, u32[]{:S(2)}) async-start(bf16[32,4,16,256]{3,2,1,0:T(8,128)(2,1)} %attend_columns.4), calls=%async_computation.1 | async-start | bytes 2097152 | tf_op jit(solution)/shard_map/cond/branch_0_fun/all_to_all | solution.py:187
where the time goes:
time: 143 us; the launch traced here: 142 us
  waiting for transfers between devices  50.7 us (35%)
  Pallas kernels  47.2 us (33%)
  starting transfers between devices  29.1 us (20%)
  blocking collectives  10.9 us (8%)
  local copies, waits for them, and re-layouts  2.98 us (2%)
    all_to_all x4, waiting for transfers between devices, exchange(): lax.all_to_all(blocks, 'grp', split_axis=0, concat_axis=0, tiled=True)  50.7 us
    pallas_call x2, Pallas kernels, attend(): pl.pallas_call(column_kernel, grid_spec=pltpu.PrefetchScalarGridSpec(num_...  36.5 us
    all_to_all x4, starting transfers between devices, exchange(): lax.all_to_all(blocks, 'grp', split_axis=0, concat_axis=0, tiled=True)  25.8 us
    all_gather x1, blocking collectives, run(): lax.all_gather(pair, 'cplx', axis=0, tiled=True, axis_index_groups=own_core)  10.9 us
    pallas_call x2, Pallas kernels, pack(): pl.pallas_call(pack_kernel, grid=(width,), in_specs=[pl.BlockSpec((comple...  6.25 us
    pallas_call x2, Pallas kernels, unpack(): pl.pallas_call(unpack_kernel, grid=(width,), in_specs=in_specs, out_specs...  4.4 us
    ppermute x1, starting transfers between devices, shards(): other = lax.ppermute(both, 'cplx', [(c, c ^ 1) for c in range(teams)])  3.33 us
  transfers between devices with their start and end apart: 5, of which 4 were waited for; matrix products, arithmetic and copies ran while one was open for 1% of the time, Pallas kernels for 29%

commit v1 on v0

v1 whole, which is shorter than its diff:
```python
from functools import partial
import math

import jax
import jax.numpy as jnp
from jax import lax
from jax.experimental import pallas as pl
from jax.experimental.pallas import tpu as pltpu
from jax.sharding import PartitionSpec as P

FOCUS_PATHS = 8
PAIRS = ((0, 2), (1, 3), (4, 6), (5, 7))
TILE = 16
SOFT_ROWS = 64
VMEM_LIMIT = 48 * 1024 * 1024
SENT = ((8,), (4, 4))
BACK = ((4, 4), (4, 4))


def swap_matrix():
    to = lax.broadcasted_iota(jnp.int32, (TILE * TILE, 1), 0)
    come = lax.broadcasted_iota(jnp.int32, (1, TILE * TILE), 1)
    return ((to & (TILE - 1)) * TILE + (to >> 4) == come).astype(jnp.bfloat16)


def swap_tokens(permutation, tokens):
    return jnp.dot(permutation, tokens, preferred_element_type=jnp.float32).astype(jnp.bfloat16)


def pack_kernel(x_ref, o_ref):
    rows, columns, channels = x_ref.shape
    homes = o_ref.shape[0]
    permutation = swap_matrix()
    for first in range(0, columns, TILE):
        tokens = x_ref[:, first : first + TILE, :].reshape(TILE * TILE, channels)
        swapped = swap_tokens(permutation, tokens)
        home = first % homes
        o_ref[home : home + TILE, first // homes] = swapped.reshape(TILE, rows, channels)


def unpack_kernel(y_ref, *rest):
    o_ref = rest[-1]
    rows, columns, channels = o_ref.shape
    homes = y_ref.shape[0]
    permutation = swap_matrix()
    for first in range(0, columns, TILE):
        home = first % homes
        tokens = y_ref[home : home + TILE, first // homes].reshape(TILE * TILE, channels)
        swapped = swap_tokens(permutation, tokens)
        o_ref[:, first : first + TILE, :] = swapped.reshape(rows, TILE, channels)


def step_of(start, width):
    return 2 if start % 2 == 0 and width % 2 == 0 else 1


def pack(rows, start, width, homes):
    complex_rows, _, channels = rows.shape
    step = step_of(start, width)
    return pl.pallas_call(
        pack_kernel,
        grid=(width // step,),
        in_specs=[
            pl.BlockSpec((complex_rows, step * homes, channels), lambda j: (0, start // step + j, 0))
        ],
        out_specs=pl.BlockSpec((homes, step, complex_rows, channels), lambda j: (0, j, 0, 0)),
        out_shape=jax.ShapeDtypeStruct((homes, width, complex_rows, channels), jnp.bfloat16),
        compiler_params=pltpu.CompilerParams(vmem_limit_bytes=VMEM_LIMIT),
        name="pack_columns",
    )(rows)


def unpack(returned, before, start, columns):
    homes, width, complex_rows, channels = returned.shape
    step = step_of(start, width)
    operands = [returned]
    in_specs = [pl.BlockSpec((homes, step, complex_rows, channels), lambda j: (0, j, 0, 0))]
    aliases = {}
    if before is not None:
        operands.append(before)
        in_specs.append(pl.BlockSpec(memory_space=pl.ANY))
        aliases = {1: 0}
    return pl.pallas_call(
        unpack_kernel,
        grid=(width // step,),
        in_specs=in_specs,
        out_specs=pl.BlockSpec(
            (complex_rows, step * homes, channels), lambda j: (0, start // step + j, 0)
        ),
        out_shape=jax.ShapeDtypeStruct((complex_rows, columns, channels), jnp.bfloat16),
        input_output_aliases=aliases,
        compiler_params=pltpu.CompilerParams(vmem_limit_bytes=VMEM_LIMIT),
        name="unpack_columns",
    )(*operands)


def column_kernel(
    depths_ref, team_ref, x_ref, parts_ref, result_ref, factor_ref, offset_ref, sigmoid_ref, shift_ref, o_ref,
    weight_ref, packed_ref, keys_ref, own_ref, scores_ref, soft_ref
):
    ranks, _, rows, channels = x_ref.shape
    seq_rows = ranks * rows
    path_dimension = channels // FOCUS_PATHS
    depth = depths_ref[team_ref[0]]

    @pl.when(pl.program_id(0) == 0)
    def _():
        width = parts_ref.shape[2]
        for part in range(parts_ref.shape[0]):
            weight_ref[:, part * width : (part + 1) * width] = parts_ref[part]

    values = x_ref[:, 0].reshape(seq_rows, channels).astype(jnp.float32)
    average = jnp.mean(values, -1, keepdims=True)
    centred = values - average
    variance = jnp.mean(jnp.square(centred), -1, keepdims=True)
    normed = (
        centred * lax.rsqrt(variance + 1e-05) * factor_ref[...] + offset_ref[...]
    ).astype(jnp.bfloat16)
    product = jnp.dot(normed, weight_ref[...], preferred_element_type=jnp.float32)
    packed_ref[:, : 3 * channels] = product[:, : 3 * channels].astype(jnp.bfloat16)
    gates = jax.nn.sigmoid(product[:, 3 * channels :] + sigmoid_ref[...])
    packed_ref[:, 3 * channels :] = gates.astype(jnp.bfloat16)

    keys_t = packed_ref[:, channels : 2 * channels].T
    lane = lax.broadcasted_iota(jnp.int32, (1, channels), 1)
    channel = lax.broadcasted_iota(jnp.int32, (channels, 1), 0)
    dead = lax.broadcasted_iota(jnp.int32, (1, seq_rows), 1) >= depth
    mask = jnp.where(dead, -1e30, 0.0).astype(jnp.bfloat16)
    for odd in range(2):
        spare = channel % (2 * path_dimension) == (1 - odd) * path_dimension
        keys_ref[odd] = jnp.where(spare, mask, keys_t)
    scaling = math.log2(math.e) / math.sqrt(path_dimension)
    half = channels // 2
    mixtures = [jnp.zeros((seq_rows, half), jnp.float32)] * 2

    def score(index):
        queries = packed_ref[:, :channels]
        for place, head in enumerate(PAIRS[index]):
            other = jnp.where(lane == (head ^ 1) * path_dimension, 1.0, 0.0).astype(jnp.bfloat16)
            own_ref[index % 2, place * seq_rows : (place + 1) * seq_rows] = jnp.where(
                lane // path_dimension == head, queries, other
            )
        scores_ref[index % 2] = jnp.dot(
            own_ref[index % 2], keys_ref[PAIRS[index][0] % 2], preferred_element_type=jnp.float32
        )

    def soften(index):
        for first in range(0, len(PAIRS[index]) * seq_rows, SOFT_ROWS):
            scores = scores_ref[index % 2, first : first + SOFT_ROWS]
            row_top = jnp.max(scores, -1, keepdims=True) * scaling
            exponent = jnp.exp2(scores * scaling - row_top)
            total = jnp.sum(exponent, -1, keepdims=True)
            soft_ref[index % 2, first : first + SOFT_ROWS] = (exponent * (1.0 / total)).astype(
                jnp.bfloat16
            )

    def mix(index):
        side = PAIRS[index][0] * path_dimension // half
        value_rows = packed_ref[:, 2 * channels + side * half : 2 * channels + (side + 1) * half]
        mixed = jnp.dot(soft_ref[index % 2], value_rows, preferred_element_type=jnp.float32)
        for place, head in enumerate(PAIRS[index]):
            own = lane[:, side * half : (side + 1) * half] // path_dimension == head
            mixtures[side] = jnp.where(
                own, mixed[place * seq_rows : (place + 1) * seq_rows], mixtures[side]
            )

    score(0)
    for index in range(len(PAIRS)):
        if index + 1 < len(PAIRS):
            score(index + 1)
        soften(index)
        if index > 0:
            mix(index - 1)
    mix(len(PAIRS) - 1)

    gate_rows = packed_ref[:, 3 * channels :].astype(jnp.float32)
    gated = (gate_rows * jnp.concatenate(mixtures, 1)).astype(jnp.bfloat16)
    update = jnp.dot(gated, result_ref[...], preferred_element_type=jnp.float32) + shift_ref[...]
    live = lax.broadcasted_iota(jnp.int32, (seq_rows, 1), 0) < depth
    update = jnp.where(live, 1.0, 0.0) * update
    changed = x_ref[:, 0].reshape(seq_rows, channels).astype(jnp.float32) + update
    o_ref[:, 0] = changed.astype(jnp.bfloat16).reshape(ranks, rows, channels)


def attend(arrived, start, width, scalars, params):
    ranks, _, rows, channels = arrived.shape
    seq_rows = ranks * rows

    def whole(a):
        return pl.BlockSpec(a.shape, lambda *_: (0,) * len(a.shape))

    return pl.pallas_call(
        column_kernel,
        grid_spec=pltpu.PrefetchScalarGridSpec(
            num_scalar_prefetch=len(scalars),
            grid=(width,),
            in_specs=[pl.BlockSpec((ranks, 1, rows, channels), lambda i, *_: (0, start + i, 0, 0))]
            + [whole(a) for a in params],
            out_specs=pl.BlockSpec((ranks, 1, rows, channels), lambda i, *_: (0, i, 0, 0)),
            scratch_shapes=[
                pltpu.VMEM((channels, 4 * channels), jnp.bfloat16),
                pltpu.VMEM((seq_rows, 4 * channels), jnp.bfloat16),
                pltpu.VMEM((2, channels, seq_rows), jnp.bfloat16),
                pltpu.VMEM((2, 2 * seq_rows, channels), jnp.bfloat16),
                pltpu.VMEM((2, 2 * seq_rows, seq_rows), jnp.float32),
                pltpu.VMEM((2, 2 * seq_rows, seq_rows), jnp.bfloat16),
            ],
        ),
        out_shape=jax.ShapeDtypeStruct((ranks, width, rows, channels), jnp.bfloat16),
        compiler_params=pltpu.CompilerParams(vmem_limit_bytes=VMEM_LIMIT),
        cost_estimate=pl.CostEstimate(
            flops=width * seq_rows * channels * (10 * channels + 4 * FOCUS_PATHS * seq_rows),
            bytes_accessed=4 * width * seq_rows * channels,
            transcendentals=width * FOCUS_PATHS * seq_rows * seq_rows,
        ),
        name="attend_columns",
    )(*scalars, arrived, *params)


def exchange(blocks):
    return lax.all_to_all(blocks, "grp", split_axis=0, concat_axis=0, tiled=True)


def chunked(rows, scalars, gathered, vectors, homes, sent, back):
    _, columns, channels = rows.shape
    later, gathered = lax.optimization_barrier((rows, gathered))
    params = (gathered[:, :channels], gathered[:, channels:].reshape(channels, channels), *vectors)
    arrived, first = [], 0
    for width in sent:
        arrived.append((first, exchange(pack(later if first else rows, first, width, homes))))
        first += width
    out, first = None, 0
    for width in back:
        begin, blocks = [a for a in arrived if a[0] <= first][-1]
        done = exchange(attend(blocks, first - begin, width, scalars, params))
        out = unpack(done, out, first, columns)
        first += width
    return out


def shards(
    sequence_stack,
    depths,
    standardize_factor,
    standardize_shift,
    input_weight,
    sigmoid_shift,
    result_matrix,
    result_shift,
):
    homes = lax.axis_size("grp")
    team = lax.axis_index("cplx")
    teams = lax.axis_size("cplx")
    vectors = [standardize_factor, standardize_shift, sigmoid_shift, result_shift]
    vectors = [vector.reshape(1, -1) for vector in vectors]
    scalars = (depths, team.astype(jnp.int32).reshape(1))
    own = (input_weight, result_matrix)
    other = lax.ppermute(own, "cplx", [(c, c ^ 1) for c in range(teams)])
    own_core = [list(range(core, teams, 2)) for core in range(2)]

    def run(core, rows, own, other):
        def flat(shard):
            return jnp.concatenate([shard[0], shard[1].reshape(-1, shard[0].shape[1])], axis=0)

        pair = jnp.stack([flat(own), flat(other)] if core == 0 else [flat(other), flat(own)])
        gathered = lax.all_gather(pair, "cplx", axis=0, tiled=True, axis_index_groups=own_core)
        return chunked(rows, scalars, gathered, vectors, homes, SENT[core], BACK[core])

    runs = [partial(run, core) for core in range(2)]
    return lax.cond(team % 2 == 0, *runs, sequence_stack[0], own, other)[None]


def solution(mesh):
    placed = (
        P("cplx", "grp", None, None),
        P(),
        P(),
        P(),
        P(None, "cplx"),
        P(),
        P("cplx", None),
        P(),
    )
    return jax.shard_map(
        shards, mesh=mesh, in_specs=placed, out_specs=P("cplx", "grp", None, None), check_vma=False
    )
```

time: 143 us -> 131 us (0.916)
  the two profiles are of different devices: /device:TPU:1 before, /device:TPU:28 now
where the time goes in v1:
time: 131 us; the launch traced here: 130 us
  waiting for transfers between devices  47.2 us (36%)
  Pallas kernels  39.8 us (30%)
  starting transfers between devices  26 us (20%)
  blocking collectives  13 us (10%)
  local copies, waits for them, and re-layouts  3.74 us (3%)
    all_to_all x3, waiting for transfers between devices, exchange(): lax.all_to_all(blocks, 'grp', split_axis=0, concat_axis=0, tiled=True)  46.2 us
    pallas_call x2, Pallas kernels, attend(): pl.pallas_call(column_kernel, grid_spec=pltpu.PrefetchScalarGridSpec(num_...  32.5 us
    all_to_all x3, starting transfers between devices, exchange(): lax.all_to_all(blocks, 'grp', split_axis=0, concat_axis=0, tiled=True)  25.5 us
    all_gather x1, blocking collectives, run(): lax.all_gather(pair, 'cplx', axis=0, tiled=True, axis_index_groups=own_core)  13 us
    pallas_call x1, Pallas kernels, pack(): pl.pallas_call(pack_kernel, grid=(width // step,), in_specs=[pl.BlockSpec...  4.31 us
    cond x26, local copies, waits for them, and re-layouts  3.62 us
    pallas_call x2, Pallas kernels, unpack(): pl.pallas_call(unpack_kernel, grid=(width // step,), in_specs=in_specs, o...  3.03 us
  transfers between devices with their start and end apart: 5, of which 4 were waited for; matrix products, arithmetic and copies ran while one was open for 0% of the time, Pallas kernels for 14%

profile of v1, /device:TPU:28, one launch (start us, length us, event | category | flops | bytes accessed | tf_op | source)
XLA Modules:
  0.0 130.1 jit_solution(7876449691465165727)
XLA Ops:
  0.0 0.0 collective-permute-start.1
  0.0 0.5 collective-permute-start
  0.5 1.0 collective-permute-done
  1.6 0.0 collective-permute-done.1
  1.6 128.6 %conditional.1 = (bf16[1,16,256,256]{3,2,1,0:T(8,128)(2,1)}) conditional(s32[]{:T(128)} %convert_element_type.3, (bf16[32,256]{1,0:T(8,128)(2,1)S(1)}, bf16[256,128]{1,0:T(8,128)(2,1)S(1)}, bf16[32,256]{1,0:T(8,128)(2,1)}, bf16[256,128]{1,0:T(8,128)(2,1)}, bf16[16,256,256]{2,1,0:T(8,128)(2,1)}, /*index=5*/s32[8]{0:T(128)}, s32[1]{0:T(128)}, ...), branch_computations={%region_0.1_spmd, %region_1.2_spmd} | conditional | flops 19864633344 | bytes 32948820 | solution.py:270
  1.6 0.0 copy-start.10
  1.6 0.6 copy-done.10
  2.2 4.3 %pack_columns.5 = bf16[32,8,16,256]{3,2,1,0:T(8,128)(2,1)} custom-call(bf16[16,256,256]{2,1,0:T(8,128)(2,1)} %get-tuple-element.68.x_ref), custom_call_target="tpu_custom_call" | custom-call | tf_op jit(solution)/shard_map/cond/branch_1_fun/pack_columns/pallas_call | solution.py:60
  6.5 0.0 copy-start.9
  6.5 0.0 copy-start.11
  6.5 0.0 copy-start.7
  6.5 11.7 %all-to-all-start.4 = ((bf16[32,8,16,256]{3,2,1,0:T(8,128)(2,1)}), bf16[32,8,16,256]{3,2,1,0:T(8,128)(2,1)S(1)}, u32[]{:S(2)}, u32[]{:S(2)}) async-start(bf16[32,8,16,256]{3,2,1,0:T(8,128)(2,1)} %pack_columns.5), calls=%async_computation.4 | async-start | bytes 4194304 | tf_op jit(solution)/shard_map/cond/branch_1_fun/all_to_all | solution.py:221
  18.2 0.0 copy-start.13
  18.2 0.0 copy-start.15
  18.2 0.0 copy-start.17
  18.3 0.0 copy-start.19
  18.3 0.0 copy-start.21
  18.3 0.0 copy-done.9
  18.3 0.0 copy-done.11
  18.3 0.0 copy-done.7
  18.4 13.0 %all_gather.5 = bf16[8,320,128]{2,1,0:T(8,128)(2,1)S(1)} all-gather(bf16[2,320,128]{2,1,0:T(8,128)(2,1)S(1)} %pad_maximum_fusion.1), channel_id=1, replica_groups={{0,64,128,192},{32,96,160,224},{1,65,129,193},{33,97,161,225},{2,66,130..., dimensions={0}, use_global_device_ids=true | all-gather | bytes 819200 | tf_op jit(solution)/shard_map/cond/branch_1_fun/all_gather | solution.py:266
  31.5 0.0 copy-start.2
  31.6 26.7 %all-to-all-done.4.x_ref = bf16[32,8,16,256]{3,2,1,0:T(8,128)(2,1)S(1)} async-done(((bf16[32,8,16,256]{3,2,1,0:T(8,128)(2,1)}), bf16[32,8,16,256]{3,2,1,0:T(8,128)(2,1)S(1)}, u32[]{:S(2)}, u32[]{:S(2)}) %all-to-all-start.4) | async-done | bytes 2097184 | tf_op jit(solution)/shard_map/cond/branch_1_fun/all_to_all | solution.py:221
  58.2 0.0 copy-done.13
  58.2 0.0 copy-done.15
  58.2 0.0 copy-done.17
  58.2 0.0 copy-done.19
  58.3 0.0 copy-done.21
  58.3 16.2 %attend_columns.7 = bf16[32,4,16,256]{3,2,1,0:T(8,128)(2,1)S(1)} custom-call(s32[8]{0:T(128)S(1)} %copy-done.21, s32[1]{0:T(128)} %get-tuple-element.67.team_ref, bf16[32,8,16,256]{3,2,1,0:T(8,128)(2,1)S(1)} %all-to-all-done.4.x_ref, bf16[8,256,128]{2,1,0:T(8,128)(2,1)S(1)} %slice.10.parts_ref, bf16[256,256]{1,0:T(8,128)(2,1)S(1)} %reshape.27.result_ref, ...), custom_call_target="tpu_custom_call" | custom-call | flops 9932111872 | bytes 2097152 | tf_op jit(solution)/shard_map/cond/branch_1_fun/attend_columns/pallas_call | solution.py:192
  74.5 0.0 copy-done.2
  74.5 0.0 copy-start.1
  74.5 1.0 copy-done.1
  75.5 6.4 %all-to-all-start.6 = ((bf16[32,4,16,256]{3,2,1,0:T(8,128)(2,1)}), bf16[32,4,16,256]{3,2,1,0:T(8,128)(2,1)S(1)}, u32[]{:S(2)}, u32[]{:S(2)}) async-start(bf16[32,4,16,256]{3,2,1,0:T(8,128)(2,1)} %copy-done.1), calls=%async_computation.6 | async-start | bytes 2097152 | tf_op jit(solution)/shard_map/cond/branch_1_fun/all_to_all | solution.py:221
  81.9 0.0 copy-start.3
  81.9 1.0 copy-done.3
  82.9 16.3 %attend_columns.6 = bf16[32,4,16,256]{3,2,1,0:T(8,128)(2,1)S(1)} custom-call(s32[8]{0:T(128)S(1)} %copy-done.21, s32[1]{0:T(128)} %get-tuple-element.67.team_ref, bf16[32,8,16,256]{3,2,1,0:T(8,128)(2,1)S(1)} %all-to-all-done.4.x_ref, bf16[8,256,128]{2,1,0:T(8,128)(2,1)S(1)} %copy-done.3, bf16[256,256]{1,0:T(8,128)(2,1)S(1)} %reshape.27.result_ref, ...), custom_call_target="tpu_custom_call" | custom-call | flops 9932111872 | bytes 2097152 | tf_op jit(solution)/shard_map/cond/branch_1_fun/attend_columns/pallas_call | solution.py:192
  99.2 0.0 copy-start
  99.2 1.0 copy-done
  100.1 2.3 %all-to-all-done.6.y_ref = bf16[32,4,16,256]{3,2,1,0:T(8,128)(2,1)S(1)} async-done(((bf16[32,4,16,256]{3,2,1,0:T(8,128)(2,1)}), bf16[32,4,16,256]{3,2,1,0:T(8,128)(2,1)S(1)}, u32[]{:S(2)}, u32[]{:S(2)}) %all-to-all-start.6) | async-done | bytes 1048608 | tf_op jit(solution)/shard_map/cond/branch_1_fun/all_to_all | solution.py:221
  102.5 7.5 %all-to-all-start.5 = ((bf16[32,4,16,256]{3,2,1,0:T(8,128)(2,1)}), bf16[32,4,16,256]{3,2,1,0:T(8,128)(2,1)S(1)}, u32[]{:S(2)}, u32[]{:S(2)}) async-start(bf16[32,4,16,256]{3,2,1,0:T(8,128)(2,1)} %copy-done), calls=%async_computation.5 | async-start | bytes 2097152 | tf_op jit(solution)/shard_map/cond/branch_1_fun/all_to_all | solution.py:221
  109.9 1.5 %unpack_columns.6.rest_0_ = bf16[16,256,256]{2,1,0:T(8,128)(2,1)} custom-call(bf16[32,4,16,256]{3,2,1,0:T(8,128)(2,1)S(1)} %all-to-all-done.6.y_ref), custom_call_target="tpu_custom_call" | custom-call | tf_op jit(solution)/shard_map/cond/branch_1_fun/unpack_columns/pallas_call | solution.py:83
  111.4 17.2 %all-to-all-done.5.y_ref = bf16[32,4,16,256]{3,2,1,0:T(8,128)(2,1)S(1)} async-done(((bf16[32,4,16,256]{3,2,1,0:T(8,128)(2,1)}), bf16[32,4,16,256]{3,2,1,0:T(8,128)(2,1)S(1)}, u32[]{:S(2)}, u32[]{:S(2)}) %all-to-all-start.5) | async-done | bytes 1048608 | tf_op jit(solution)/shard_map/cond/branch_1_fun/all_to_all | solution.py:221
  128.6 1.5 %unpack_columns.7 = bf16[16,256,256]{2,1,0:T(8,128)(2,1)} custom-call(bf16[32,4,16,256]{3,2,1,0:T(8,128)(2,1)S(1)} %all-to-all-done.5.y_ref, bf16[16,256,256]{2,1,0:T(8,128)(2,1)} %unpack_columns.6.rest_0_), custom_call_target="tpu_custom_call", output_to_operand_aliasing={{}: (1, {})} | custom-call | tf_op jit(solution)/shard_map/cond/branch_1_fun/unpack_columns/pallas_call | solution.py:83
  (7 shorter events, 0.1 us)
Async XLA Ops:
  0.0 1.6 %collective-permute-start.1 = (bf16[256,128]{1,0:T(8,128)(2,1)}, bf16[256,128]{1,0:T(8,128)(2,1)S(1)}, u32[]{:S(2)}, u32[]{:S(2)}) collective-permute-start(bf16[256,128]{1,0:T(8,128)(2,1)} %param.14), channel_id=1, source_target_pairs={{0,32},{32,0},{64,96},{96,64},{128,160},{160,128},{192,224},{224,1... | collective-permute-start | bytes 196616 | tf_op jit(solution)/shard_map/ppermute | solution.py:258
  0.0 1.6 %collective-permute-start = (bf16[32,256]{1,0:T(8,128)(2,1)}, bf16[32,256]{1,0:T(8,128)(2,1)S(1)}, u32[]{:S(2)}, u32[]{:S(2)}) collective-permute-start(bf16[32,256]{1,0:T(8,128)(2,1)} %param.16), channel_id=1, source_target_pairs={{0,32},{32,0},{64,96},{96,64},{128,160},{160,128},{192,224},{224,1... | collective-permute-start | bytes 49160 | tf_op jit(solution)/shard_map/ppermute | solution.py:258
  1.6 0.6 copy-start.10
  6.5 11.8 %copy-start.9 = (bf16[32,256]{1,0:T(8,128)(2,1)S(1)}, bf16[32,256]{1,0:T(8,128)(2,1)}, u32[]{:S(2)}) copy-start(bf16[32,256]{1,0:T(8,128)(2,1)} %get-tuple-element.70) | copy-start | bytes 49156 | tf_op jit(solution)/shard_map/cond
  6.5 11.8 %copy-start.11 = (bf16[32,256]{1,0:T(8,128)(2,1)S(1)}, bf16[32,256]{1,0:T(8,128)(2,1)}, u32[]{:S(2)}) copy-start(bf16[32,256]{1,0:T(8,128)(2,1)} %copy-done.10) | copy-start | bytes 49156 | tf_op jit(solution)/shard_map/cond
  6.5 11.9 %copy-start.7 = (bf16[256,128]{1,0:T(8,128)(2,1)S(1)}, bf16[256,128]{1,0:T(8,128)(2,1)}, u32[]{:S(2)}) copy-start(bf16[256,128]{1,0:T(8,128)(2,1)} %get-tuple-element.69) | copy-start | bytes 196612 | tf_op jit(solution)/shard_map/cond
  6.5 51.8 %all-to-all-start.4 = ((bf16[32,8,16,256]{3,2,1,0:T(8,128)(2,1)}), bf16[32,8,16,256]{3,2,1,0:T(8,128)(2,1)S(1)}, u32[]{:S(2)}, u32[]{:S(2)}) async-start(bf16[32,8,16,256]{3,2,1,0:T(8,128)(2,1)} %pack_columns.5), calls=%async_computation.4 | async-start | bytes 4194304 | tf_op jit(solution)/shard_map/cond/branch_1_fun/all_to_all | solution.py:221
  18.2 40.0 %copy-start.13 = (f32[1,256]{1,0:T(1,128)S(1)}, f32[1,256]{1,0:T(1,128)}, u32[]{:S(2)}) copy-start(f32[1,256]{1,0:T(1,128)} %get-tuple-element.74.factor_ref) | copy-start | bytes 3076 | tf_op jit(solution)/shard_map/cond
  18.2 40.0 %copy-start.15 = (f32[1,256]{1,0:T(1,128)S(1)}, f32[1,256]{1,0:T(1,128)}, u32[]{:S(2)}) copy-start(f32[1,256]{1,0:T(1,128)} %get-tuple-element.75.offset_ref) | copy-start | bytes 3076 | tf_op jit(solution)/shard_map/cond
  18.2 40.0 %copy-start.17 = (f32[1,256]{1,0:T(1,128)S(1)}, f32[1,256]{1,0:T(1,128)}, u32[]{:S(2)}) copy-start(f32[1,256]{1,0:T(1,128)} %get-tuple-element.76.sigmoid_ref) | copy-start | bytes 3076 | tf_op jit(solution)/shard_map/cond
  18.3 40.0 %copy-start.19 = (f32[1,256]{1,0:T(1,128)S(1)}, f32[1,256]{1,0:T(1,128)}, u32[]{:S(2)}) copy-start(f32[1,256]{1,0:T(1,128)} %get-tuple-element.77.shift_ref) | copy-start | bytes 3076 | tf_op jit(solution)/shard_map/cond
  18.3 40.0 %copy-start.21 = (s32[8]{0:T(128)S(1)}, s32[8]{0:T(128)}, u32[]{:S(2)}) copy-start(s32[8]{0:T(128)} %get-tuple-element.66.depths_ref) | copy-start | bytes 100 | tf_op jit(solution)/shard_map/cond
  31.5 43.0 %copy-start.2 = (bf16[8,256,128]{2,1,0:T(8,128)(2,1)}, bf16[8,256,128]{2,1,0:T(8,128)(2,1)S(1)}, u32[]{:S(2)}) copy-start(bf16[8,256,128]{2,1,0:T(8,128)(2,1)S(1)} %slice.10.parts_ref) | copy-start | bytes 1572868 | tf_op jit(solution)/shard_map/cond
  74.5 1.0 copy-start.1
  75.5 27.0 %all-to-all-start.6 = ((bf16[32,4,16,256]{3,2,1,0:T(8,128)(2,1)}), bf16[32,4,16,256]{3,2,1,0:T(8,128)(2,1)S(1)}, u32[]{:S(2)}, u32[]{:S(2)}) async-start(bf16[32,4,16,256]{3,2,1,0:T(8,128)(2,1)} %copy-done.1), calls=%async_computation.6 | async-start | bytes 2097152 | tf_op jit(solution)/shard_map/cond/branch_1_fun/all_to_all | solution.py:221
  81.9 1.0 copy-start.3
  99.2 1.0 copy-start
  102.5 26.2 %all-to-all-start.5 = ((bf16[32,4,16,256]{3,2,1,0:T(8,128)(2,1)}), bf16[32,4,16,256]{3,2,1,0:T(8,128)(2,1)S(1)}, u32[]{:S(2)}, u32[]{:S(2)}) async-start(bf16[32,4,16,256]{3,2,1,0:T(8,128)(2,1)} %copy-done), calls=%async_computation.5 | async-start | bytes 2097152 | tf_op jit(solution)/shard_map/cond/branch_1_fun/all_to_all | solution.py:221

commit v2 on v1

--- a/solution.py
+++ b/solution.py
@@ -12,7 +12,8 @@
 PAIRS = ((0, 2), (1, 3), (4, 6), (5, 7))
 TILE = 16
 SOFT_ROWS = 64
-VMEM_LIMIT = 48 * 1024 * 1024
+VMEM_LIMIT = 32 * 1024 * 1024
+AT_ONCE = (1, 1)
 SENT = ((8,), (4, 4))
 BACK = ((4, 4), (4, 4))
 
@@ -95,7 +96,7 @@
 
 
 def column_kernel(
-    depths_ref, team_ref, x_ref, parts_ref, result_ref, factor_ref, offset_ref, sigmoid_ref, shift_ref, o_ref,
+    columns, depths_ref, team_ref, x_ref, parts_ref, result_ref, factor_ref, offset_ref, sigmoid_ref, shift_ref, o_ref,
     weight_ref, packed_ref, keys_ref, own_ref, scores_ref, soft_ref
 ):
     ranks, _, rows, channels = x_ref.shape
@@ -109,43 +110,47 @@
         for part in range(parts_ref.shape[0]):
             weight_ref[:, part * width : (part + 1) * width] = parts_ref[part]
 
-    values = x_ref[:, 0].reshape(seq_rows, channels).astype(jnp.float32)
-    average = jnp.mean(values, -1, keepdims=True)
-    centred = values - average
-    variance = jnp.mean(jnp.square(centred), -1, keepdims=True)
-    normed = (
-        centred * lax.rsqrt(variance + 1e-05) * factor_ref[...] + offset_ref[...]
-    ).astype(jnp.bfloat16)
-    product = jnp.dot(normed, weight_ref[...], preferred_element_type=jnp.float32)
-    packed_ref[:, : 3 * channels] = product[:, : 3 * channels].astype(jnp.bfloat16)
-    gates = jax.nn.sigmoid(product[:, 3 * channels :] + sigmoid_ref[...])
-    packed_ref[:, 3 * channels :] = gates.astype(jnp.bfloat16)
-
-    keys_t = packed_ref[:, channels : 2 * channels].T
     lane = lax.broadcasted_iota(jnp.int32, (1, channels), 1)
     channel = lax.broadcasted_iota(jnp.int32, (channels, 1), 0)
     dead = lax.broadcasted_iota(jnp.int32, (1, seq_rows), 1) >= depth
     mask = jnp.where(dead, -1e30, 0.0).astype(jnp.bfloat16)
-    for odd in range(2):
-        spare = channel % (2 * path_dimension) == (1 - odd) * path_dimension
-        keys_ref[odd] = jnp.where(spare, mask, keys_t)
     scaling = math.log2(math.e) / math.sqrt(path_dimension)
     half = channels // 2
-    mixtures = [jnp.zeros((seq_rows, half), jnp.float32)] * 2
+    count = len(PAIRS)
+    mixtures = [[jnp.zeros((seq_rows, half), jnp.float32)] * 2 for _ in range(columns)]
+
+    def project(column):
+        values = x_ref[:, column].reshape(seq_rows, channels).astype(jnp.float32)
+        average = jnp.mean(values, -1, keepdims=True)
+        centred = values - average
+        variance = jnp.mean(jnp.square(centred), -1, keepdims=True)
+        normed = (
+            centred * lax.rsqrt(variance + 1e-05) * factor_ref[...] + offset_ref[...]
+        ).astype(jnp.bfloat16)
+        product = jnp.dot(normed, weight_ref[...], preferred_element_type=jnp.float32)
+        packed_ref[column, :, : 3 * channels] = product[:, : 3 * channels].astype(jnp.bfloat16)
+        gates = jax.nn.sigmoid(product[:, 3 * channels :] + sigmoid_ref[...])
+        packed_ref[column, :, 3 * channels :] = gates.astype(jnp.bfloat16)
+
+        keys_t = packed_ref[column, :, channels : 2 * channels].T
+        for odd in range(2):
+            spare = channel % (2 * path_dimension) == (1 - odd) * path_dimension
+            keys_ref[column, odd] = jnp.where(spare, mask, keys_t)
 
     def score(index):
-        queries = packed_ref[:, :channels]
-        for place, head in enumerate(PAIRS[index]):
+        column, pair = index // count, PAIRS[index % count]
+        queries = packed_ref[column, :, :channels]
+        for place, head in enumerate(pair):
             other = jnp.where(lane == (head ^ 1) * path_dimension, 1.0, 0.0).astype(jnp.bfloat16)
             own_ref[index % 2, place * seq_rows : (place + 1) * seq_rows] = jnp.where(
                 lane // path_dimension == head, queries, other
             )
         scores_ref[index % 2] = jnp.dot(
-            own_ref[index % 2], keys_ref[PAIRS[index][0] % 2], preferred_element_type=jnp.float32
+            own_ref[index % 2], keys_ref[column, pair[0] % 2], preferred_element_type=jnp.float32
         )
 
     def soften(index):
-        for first in range(0, len(PAIRS[index]) * seq_rows, SOFT_ROWS):
+        for first in range(0, len(PAIRS[0]) * seq_rows, SOFT_ROWS):
             scores = scores_ref[index % 2, first : first + SOFT_ROWS]
             row_top = jnp.max(scores, -1, keepdims=True) * scaling
             exponent = jnp.exp2(scores * scaling - row_top)
@@ -155,34 +160,44 @@
             )
 
     def mix(index):
-        side = PAIRS[index][0] * path_dimension // half
-        value_rows = packed_ref[:, 2 * channels + side * half : 2 * channels + (side + 1) * half]
+        column, pair = index // count, PAIRS[index % count]
+        side = pair[0] * path_dimension // half
+        value_rows = packed_ref[column, :, 2 * channels + side * half : 2 * channels + (side + 1) * half]
         mixed = jnp.dot(soft_ref[index % 2], value_rows, preferred_element_type=jnp.float32)
-        for place, head in enumerate(PAIRS[index]):
+        for place, head in enumerate(pair):
             own = lane[:, side * half : (side + 1) * half] // path_dimension == head
-            mixtures[side] = jnp.where(
-                own, mixed[place * seq_rows : (place + 1) * seq_rows], mixtures[side]
+            mixtures[column][side] = jnp.where(
+                own, mixed[place * seq_rows : (place + 1) * seq_rows], mixtures[column][side]
             )
 
+    def finish(column):
+        gate_rows = packed_ref[column, :, 3 * channels :].astype(jnp.float32)
+        gated = (gate_rows * jnp.concatenate(mixtures[column], 1)).astype(jnp.bfloat16)
+        update = jnp.dot(gated, result_ref[...], preferred_element_type=jnp.float32) + shift_ref[...]
+        live = lax.broadcasted_iota(jnp.int32, (seq_rows, 1), 0) < depth
+        update = jnp.where(live, 1.0, 0.0) * update
+        changed = x_ref[:, column].reshape(seq_rows, channels).astype(jnp.float32) + update
+        o_ref[:, column] = changed.astype(jnp.bfloat16).reshape(ranks, rows, channels)
+
+    project(0)
     score(0)
-    for index in range(len(PAIRS)):
-        if index + 1 < len(PAIRS):
-            score(index + 1)
+    total_count = columns * count
+    for index in range(total_count):
+        following = index + 1
+        if following < total_count:
+            score(following)
+            if index % count == 1 and index // count + 1 < columns:
+                project(index // count + 1)
         soften(index)
         if index > 0:
             mix(index - 1)
-    mix(len(PAIRS) - 1)
-
-    gate_rows = packed_ref[:, 3 * channels :].astype(jnp.float32)
-    gated = (gate_rows * jnp.concatenate(mixtures, 1)).astype(jnp.bfloat16)
-    update = jnp.dot(gated, result_ref[...], preferred_element_type=jnp.float32) + shift_ref[...]
-    live = lax.broadcasted_iota(jnp.int32, (seq_rows, 1), 0) < depth
-    update = jnp.where(live, 1.0, 0.0) * update
-    changed = x_ref[:, 0].reshape(seq_rows, channels).astype(jnp.float32) + update
-    o_ref[:, 0] = changed.astype(jnp.bfloat16).reshape(ranks, rows, channels)
-
-
-def attend(arrived, start, width, scalars, params):
+            if index % count == 0:
+                finish(index // count - 1)
+    mix(total_count - 1)
+    finish(columns - 1)
+
+
+def attend(arrived, start, width, columns, scalars, params):
     ranks, _, rows, channels = arrived.shape
     seq_rows = ranks * rows
 
@@ -190,17 +205,19 @@
         return pl.BlockSpec(a.shape, lambda *_: (0,) * len(a.shape))
 
     return pl.pallas_call(
-        column_kernel,
+        partial(column_kernel, columns),
         grid_spec=pltpu.PrefetchScalarGridSpec(
             num_scalar_prefetch=len(scalars),
-            grid=(width,),
-            in_specs=[pl.BlockSpec((ranks, 1, rows, channels), lambda i, *_: (0, start + i, 0, 0))]
+            grid=(width // columns,),
+            in_specs=[
+                pl.BlockSpec((ranks, columns, rows, channels), lambda i, *_: (0, start // columns + i, 0, 0))
+            ]
             + [whole(a) for a in params],
-            out_specs=pl.BlockSpec((ranks, 1, rows, channels), lambda i, *_: (0, i, 0, 0)),
+            out_specs=pl.BlockSpec((ranks, columns, rows, channels), lambda i, *_: (0, i, 0, 0)),
             scratch_shapes=[
                 pltpu.VMEM((channels, 4 * channels), jnp.bfloat16),
-                pltpu.VMEM((seq_rows, 4 * channels), jnp.bfloat16),
-                pltpu.VMEM((2, channels, seq_rows), jnp.bfloat16),
+                pltpu.VMEM((columns, seq_rows, 4 * channels), jnp.bfloat16),
+                pltpu.VMEM((columns, 2, channels, seq_rows), jnp.bfloat16),
                 pltpu.VMEM((2, 2 * seq_rows, channels), jnp.bfloat16),
                 pltpu.VMEM((2, 2 * seq_rows, seq_rows), jnp.float32),
                 pltpu.VMEM((2, 2 * seq_rows, seq_rows), jnp.bfloat16),
@@ -221,18 +238,18 @@
     return lax.all_to_all(blocks, "grp", split_axis=0, concat_axis=0, tiled=True)
 
 
-def chunked(rows, scalars, gathered, vectors, homes, sent, back):
+def chunked(rows, scalars, gathered, vectors, homes, core):
     _, columns, channels = rows.shape
     later, gathered = lax.optimization_barrier((rows, gathered))
     params = (gathered[:, :channels], gathered[:, channels:].reshape(channels, channels), *vectors)
     arrived, first = [], 0
-    for width in sent:
+    for width in SENT[core]:
         arrived.append((first, exchange(pack(later if first else rows, first, width, homes))))
         first += width
     out, first = None, 0
-    for width in back:
+    for width in BACK[core]:
         begin, blocks = [a for a in arrived if a[0] <= first][-1]
-        done = exchange(attend(blocks, first - begin, width, scalars, params))
+        done = exchange(attend(blocks, first - begin, width, AT_ONCE[core], scalars, params))
         out = unpack(done, out, first, columns)
         first += width
     return out
@@ -264,7 +281,7 @@
 
         pair = jnp.stack([flat(own), flat(other)] if core == 0 else [flat(other), flat(own)])
         gathered = lax.all_gather(pair, "cplx", axis=0, tiled=True, axis_index_groups=own_core)
-        return chunked(rows, scalars, gathered, vectors, homes, SENT[core], BACK[core])
+        return chunked(rows, scalars, gathered, vectors, homes, core)
 
     runs = [partial(run, core) for core in range(2)]
     return lax.cond(team % 2 == 0, *runs, sequence_stack[0], own, other)[None]

time: 131 us -> 131 us (level)
  no operation moved by 1% of the time
where the time goes in v2:
time: 131 us; the launch traced here: 130 us
  waiting for transfers between devices  47.2 us (36%)
  Pallas kernels  39.8 us (30%)
  starting transfers between devices  26.1 us (20%)
  blocking collectives  13 us (10%)
  local copies, waits for them, and re-layouts  3.74 us (3%)
    all_to_all x3, waiting for transfers between devices, exchange(): lax.all_to_all(blocks, 'grp', split_axis=0, concat_axis=0, tiled=True)  46.2 us
    pallas_call x2, Pallas kernels, attend(): pl.pallas_call(partial(column_kernel, columns), grid_spec=pltpu.PrefetchS...  32.5 us
    all_to_all x3, starting transfers between devices, exchange(): lax.all_to_all(blocks, 'grp', split_axis=0, concat_axis=0, tiled=True)  25.5 us
    all_gather x1, blocking collectives, run(): lax.all_gather(pair, 'cplx', axis=0, tiled=True, axis_index_groups=own_core)  13 us
    pallas_call x1, Pallas kernels, pack(): pl.pallas_call(pack_kernel, grid=(width // step,), in_specs=[pl.BlockSpec...  4.31 us
    cond x26, local copies, waits for them, and re-layouts  3.62 us
    pallas_call x2, Pallas kernels, unpack(): pl.pallas_call(unpack_kernel, grid=(width // step,), in_specs=in_specs, o...  3.03 us
  transfers between devices with their start and end apart: 5, of which 4 were waited for; matrix products, arithmetic and copies ran while one was open for 0% of the time, Pallas kernels for 14%

profile of v2, /device:TPU:28, one launch (start us, length us, event | category | flops | bytes accessed | tf_op | source)
XLA Modules:
  0.0 130.1 jit_solution(5545235387315016026)
XLA Ops:
  0.0 0.0 collective-permute-start.1
  0.0 0.5 collective-permute-start
  0.5 1.0 collective-permute-done
  1.6 0.0 collective-permute-done.1
  1.6 128.6 %conditional.1 = (bf16[1,16,256,256]{3,2,1,0:T(8,128)(2,1)}) conditional(s32[]{:T(128)} %convert_element_type.3, (bf16[32,256]{1,0:T(8,128)(2,1)S(1)}, bf16[256,128]{1,0:T(8,128)(2,1)S(1)}, bf16[32,256]{1,0:T(8,128)(2,1)}, bf16[256,128]{1,0:T(8,128)(2,1)}, bf16[16,256,256]{2,1,0:T(8,128)(2,1)}, /*index=5*/s32[8]{0:T(128)}, s32[1]{0:T(128)}, ...), branch_computations={%region_0.1_spmd, %region_1.2_spmd} | conditional | flops 19864633344 | bytes 32948820 | solution.py:287
  1.6 0.0 copy-start.10
  1.6 0.6 copy-done.10
  2.2 4.3 %pack_columns.5 = bf16[32,8,16,256]{3,2,1,0:T(8,128)(2,1)} custom-call(bf16[16,256,256]{2,1,0:T(8,128)(2,1)} %get-tuple-element.68.x_ref), custom_call_target="tpu_custom_call" | custom-call | tf_op jit(solution)/shard_map/cond/branch_1_fun/pack_columns/pallas_call | solution.py:61
  6.5 0.0 copy-start.9
  6.5 0.0 copy-start.11
  6.5 0.0 copy-start.7
  6.5 11.7 %all-to-all-start.4 = ((bf16[32,8,16,256]{3,2,1,0:T(8,128)(2,1)}), bf16[32,8,16,256]{3,2,1,0:T(8,128)(2,1)S(1)}, u32[]{:S(2)}, u32[]{:S(2)}) async-start(bf16[32,8,16,256]{3,2,1,0:T(8,128)(2,1)} %pack_columns.5), calls=%async_computation.4 | async-start | bytes 4194304 | tf_op jit(solution)/shard_map/cond/branch_1_fun/all_to_all | solution.py:238
  18.2 0.0 copy-start.13
  18.2 0.0 copy-start.15
  18.2 0.0 copy-start.17
  18.3 0.0 copy-start.19
  18.3 0.0 copy-start.21
  18.3 0.0 copy-done.9
  18.3 0.0 copy-done.11
  18.3 0.0 copy-done.7
  18.4 13.0 %all_gather.5 = bf16[8,320,128]{2,1,0:T(8,128)(2,1)S(1)} all-gather(bf16[2,320,128]{2,1,0:T(8,128)(2,1)S(1)} %pad_maximum_fusion.1), channel_id=1, replica_groups={{0,64,128,192},{32,96,160,224},{1,65,129,193},{33,97,161,225},{2,66,130..., dimensions={0}, use_global_device_ids=true | all-gather | bytes 819200 | tf_op jit(solution)/shard_map/cond/branch_1_fun/all_gather | solution.py:283
  31.5 0.0 copy-start.2
  31.6 26.7 %all-to-all-done.4.x_ref = bf16[32,8,16,256]{3,2,1,0:T(8,128)(2,1)S(1)} async-done(((bf16[32,8,16,256]{3,2,1,0:T(8,128)(2,1)}), bf16[32,8,16,256]{3,2,1,0:T(8,128)(2,1)S(1)}, u32[]{:S(2)}, u32[]{:S(2)}) %all-to-all-start.4) | async-done | bytes 2097184 | tf_op jit(solution)/shard_map/cond/branch_1_fun/all_to_all | solution.py:238
  58.2 0.0 copy-done.13
  58.2 0.0 copy-done.15
  58.2 0.0 copy-done.17
  58.2 0.0 copy-done.19
  58.3 0.0 copy-done.21
  58.3 16.2 %attend_columns.7 = bf16[32,4,16,256]{3,2,1,0:T(8,128)(2,1)S(1)} custom-call(s32[8]{0:T(128)S(1)} %copy-done.21, s32[1]{0:T(128)} %get-tuple-element.67.team_ref, bf16[32,8,16,256]{3,2,1,0:T(8,128)(2,1)S(1)} %all-to-all-done.4.x_ref, bf16[8,256,128]{2,1,0:T(8,128)(2,1)S(1)} %slice.10.parts_ref, bf16[256,256]{1,0:T(8,128)(2,1)S(1)} %reshape.27.result_ref, ...), custom_call_target="tpu_custom_call" | custom-call | flops 9932111872 | bytes 2097152 | tf_op jit(solution)/shard_map/cond/branch_1_fun/attend_columns/pallas_call | solution.py:207
  74.5 0.0 copy-done.2
  74.5 0.0 copy-start.1
  74.5 1.0 copy-done.1
  75.5 6.4 %all-to-all-start.6 = ((bf16[32,4,16,256]{3,2,1,0:T(8,128)(2,1)}), bf16[32,4,16,256]{3,2,1,0:T(8,128)(2,1)S(1)}, u32[]{:S(2)}, u32[]{:S(2)}) async-start(bf16[32,4,16,256]{3,2,1,0:T(8,128)(2,1)} %copy-done.1), calls=%async_computation.6 | async-start | bytes 2097152 | tf_op jit(solution)/shard_map/cond/branch_1_fun/all_to_all | solution.py:238
  81.9 0.0 copy-start.3
  81.9 1.0 copy-done.3
  82.9 16.2 %attend_columns.6 = bf16[32,4,16,256]{3,2,1,0:T(8,128)(2,1)S(1)} custom-call(s32[8]{0:T(128)S(1)} %copy-done.21, s32[1]{0:T(128)} %get-tuple-element.67.team_ref, bf16[32,8,16,256]{3,2,1,0:T(8,128)(2,1)S(1)} %all-to-all-done.4.x_ref, bf16[8,256,128]{2,1,0:T(8,128)(2,1)S(1)} %copy-done.3, bf16[256,256]{1,0:T(8,128)(2,1)S(1)} %reshape.27.result_ref, ...), custom_call_target="tpu_custom_call" | custom-call | flops 9932111872 | bytes 2097152 | tf_op jit(solution)/shard_map/cond/branch_1_fun/attend_columns/pallas_call | solution.py:207
  99.1 0.0 copy-start
  99.2 1.0 copy-done
  100.1 2.3 %all-to-all-done.6.y_ref = bf16[32,4,16,256]{3,2,1,0:T(8,128)(2,1)S(1)} async-done(((bf16[32,4,16,256]{3,2,1,0:T(8,128)(2,1)}), bf16[32,4,16,256]{3,2,1,0:T(8,128)(2,1)S(1)}, u32[]{:S(2)}, u32[]{:S(2)}) %all-to-all-start.6) | async-done | bytes 1048608 | tf_op jit(solution)/shard_map/cond/branch_1_fun/all_to_all | solution.py:238
  102.5 7.5 %all-to-all-start.5 = ((bf16[32,4,16,256]{3,2,1,0:T(8,128)(2,1)}), bf16[32,4,16,256]{3,2,1,0:T(8,128)(2,1)S(1)}, u32[]{:S(2)}, u32[]{:S(2)}) async-start(bf16[32,4,16,256]{3,2,1,0:T(8,128)(2,1)} %copy-done), calls=%async_computation.5 | async-start | bytes 2097152 | tf_op jit(solution)/shard_map/cond/branch_1_fun/all_to_all | solution.py:238
  109.9 1.5 %unpack_columns.6.rest_0_ = bf16[16,256,256]{2,1,0:T(8,128)(2,1)} custom-call(bf16[32,4,16,256]{3,2,1,0:T(8,128)(2,1)S(1)} %all-to-all-done.6.y_ref), custom_call_target="tpu_custom_call" | custom-call | tf_op jit(solution)/shard_map/cond/branch_1_fun/unpack_columns/pallas_call | solution.py:84
  111.5 17.2 %all-to-all-done.5.y_ref = bf16[32,4,16,256]{3,2,1,0:T(8,128)(2,1)S(1)} async-done(((bf16[32,4,16,256]{3,2,1,0:T(8,128)(2,1)}), bf16[32,4,16,256]{3,2,1,0:T(8,128)(2,1)S(1)}, u32[]{:S(2)}, u32[]{:S(2)}) %all-to-all-start.5) | async-done | bytes 1048608 | tf_op jit(solution)/shard_map/cond/branch_1_fun/all_to_all | solution.py:238
  128.6 1.5 %unpack_columns.7 = bf16[16,256,256]{2,1,0:T(8,128)(2,1)} custom-call(bf16[32,4,16,256]{3,2,1,0:T(8,128)(2,1)S(1)} %all-to-all-done.5.y_ref, bf16[16,256,256]{2,1,0:T(8,128)(2,1)} %unpack_columns.6.rest_0_), custom_call_target="tpu_custom_call", output_to_operand_aliasing={{}: (1, {})} | custom-call | tf_op jit(solution)/shard_map/cond/branch_1_fun/unpack_columns/pallas_call | solution.py:84
  (7 shorter events, 0.1 us)
Async XLA Ops:
  0.0 1.6 %collective-permute-start.1 = (bf16[256,128]{1,0:T(8,128)(2,1)}, bf16[256,128]{1,0:T(8,128)(2,1)S(1)}, u32[]{:S(2)}, u32[]{:S(2)}) collective-permute-start(bf16[256,128]{1,0:T(8,128)(2,1)} %param.14), channel_id=1, source_target_pairs={{0,32},{32,0},{64,96},{96,64},{128,160},{160,128},{192,224},{224,1... | collective-permute-start | bytes 196616 | tf_op jit(solution)/shard_map/ppermute | solution.py:275
  0.0 1.6 %collective-permute-start = (bf16[32,256]{1,0:T(8,128)(2,1)}, bf16[32,256]{1,0:T(8,128)(2,1)S(1)}, u32[]{:S(2)}, u32[]{:S(2)}) collective-permute-start(bf16[32,256]{1,0:T(8,128)(2,1)} %param.16), channel_id=1, source_target_pairs={{0,32},{32,0},{64,96},{96,64},{128,160},{160,128},{192,224},{224,1... | collective-permute-start | bytes 49160 | tf_op jit(solution)/shard_map/ppermute | solution.py:275
  1.6 0.6 copy-start.10
  6.5 11.8 %copy-start.9 = (bf16[32,256]{1,0:T(8,128)(2,1)S(1)}, bf16[32,256]{1,0:T(8,128)(2,1)}, u32[]{:S(2)}) copy-start(bf16[32,256]{1,0:T(8,128)(2,1)} %get-tuple-element.70) | copy-start | bytes 49156 | tf_op jit(solution)/shard_map/cond
  6.5 11.8 %copy-start.11 = (bf16[32,256]{1,0:T(8,128)(2,1)S(1)}, bf16[32,256]{1,0:T(8,128)(2,1)}, u32[]{:S(2)}) copy-start(bf16[32,256]{1,0:T(8,128)(2,1)} %copy-done.10) | copy-start | bytes 49156 | tf_op jit(solution)/shard_map/cond
  6.5 11.9 %copy-start.7 = (bf16[256,128]{1,0:T(8,128)(2,1)S(1)}, bf16[256,128]{1,0:T(8,128)(2,1)}, u32[]{:S(2)}) copy-start(bf16[256,128]{1,0:T(8,128)(2,1)} %get-tuple-element.69) | copy-start | bytes 196612 | tf_op jit(solution)/shard_map/cond
  6.5 51.8 %all-to-all-start.4 = ((bf16[32,8,16,256]{3,2,1,0:T(8,128)(2,1)}), bf16[32,8,16,256]{3,2,1,0:T(8,128)(2,1)S(1)}, u32[]{:S(2)}, u32[]{:S(2)}) async-start(bf16[32,8,16,256]{3,2,1,0:T(8,128)(2,1)} %pack_columns.5), calls=%async_computation.4 | async-start | bytes 4194304 | tf_op jit(solution)/shard_map/cond/branch_1_fun/all_to_all | solution.py:238
  18.2 40.0 %copy-start.13 = (f32[1,256]{1,0:T(1,128)S(1)}, f32[1,256]{1,0:T(1,128)}, u32[]{:S(2)}) copy-start(f32[1,256]{1,0:T(1,128)} %get-tuple-element.74.factor_ref) | copy-start | bytes 3076 | tf_op jit(solution)/shard_map/cond
  18.2 40.0 %copy-start.15 = (f32[1,256]{1,0:T(1,128)S(1)}, f32[1,256]{1,0:T(1,128)}, u32[]{:S(2)}) copy-start(f32[1,256]{1,0:T(1,128)} %get-tuple-element.75.offset_ref) | copy-start | bytes 3076 | tf_op jit(solution)/shard_map/cond
  18.2 40.0 %copy-start.17 = (f32[1,256]{1,0:T(1,128)S(1)}, f32[1,256]{1,0:T(1,128)}, u32[]{:S(2)}) copy-start(f32[1,256]{1,0:T(1,128)} %get-tuple-element.76.sigmoid_ref) | copy-start | bytes 3076 | tf_op jit(solution)/shard_map/cond
  18.3 40.0 %copy-start.19 = (f32[1,256]{1,0:T(1,128)S(1)}, f32[1,256]{1,0:T(1,128)}, u32[]{:S(2)}) copy-start(f32[1,256]{1,0:T(1,128)} %get-tuple-element.77.shift_ref) | copy-start | bytes 3076 | tf_op jit(solution)/shard_map/cond
  18.3 40.0 %copy-start.21 = (s32[8]{0:T(128)S(1)}, s32[8]{0:T(128)}, u32[]{:S(2)}) copy-start(s32[8]{0:T(128)} %get-tuple-element.66.depths_ref) | copy-start | bytes 100 | tf_op jit(solution)/shard_map/cond
  31.5 43.0 %copy-start.2 = (bf16[8,256,128]{2,1,0:T(8,128)(2,1)}, bf16[8,256,128]{2,1,0:T(8,128)(2,1)S(1)}, u32[]{:S(2)}) copy-start(bf16[8,256,128]{2,1,0:T(8,128)(2,1)S(1)} %slice.10.parts_ref) | copy-start | bytes 1572868 | tf_op jit(solution)/shard_map/cond
  74.5 1.0 copy-start.1
  75.5 27.0 %all-to-all-start.6 = ((bf16[32,4,16,256]{3,2,1,0:T(8,128)(2,1)}), bf16[32,4,16,256]{3,2,1,0:T(8,128)(2,1)S(1)}, u32[]{:S(2)}, u32[]{:S(2)}) async-start(bf16[32,4,16,256]{3,2,1,0:T(8,128)(2,1)} %copy-done.1), calls=%async_computation.6 | async-start | bytes 2097152 | tf_op jit(solution)/shard_map/cond/branch_1_fun/all_to_all | solution.py:238
  81.9 1.0 copy-start.3
  99.1 1.0 copy-start
  102.5 26.2 %all-to-all-start.5 = ((bf16[32,4,16,256]{3,2,1,0:T(8,128)(2,1)}), bf16[32,4,16,256]{3,2,1,0:T(8,128)(2,1)S(1)}, u32[]{:S(2)}, u32[]{:S(2)}) async-start(bf16[32,4,16,256]{3,2,1,0:T(8,128)(2,1)} %copy-done), calls=%async_computation.5 | async-start | bytes 2097152 | tf_op jit(solution)/shard_map/cond/branch_1_fun/all_to_all | solution.py:238
